TPU v7x, 32 devices: a whole 2x2x4 slice. The times are simulated.
32 devices in a mesh: seq: 16 (over z, y, core), kv: 2 (over x).
Axes of the slice: x: 2, y: 2, z: 4, core: 2. Of those that a mesh axis runs over, the one named last changes fastest.
Arguments:
- plan: int32 [16], replicated, may hold values from 0 to 15, each once
- queries: bfloat16 [2048, 1024], P('seq', 'kv'), may hold values from -24 to 24
- keys: bfloat16 [2048, 256], P('seq', 'kv'), may hold values from -9 to 9
- student_c: bfloat16 [2048, 1024], P('seq', 'kv'), may hold values from -0.125 to 0.125
- layer_input: bfloat16 [2048, 8192], P('seq', 'kv'), may hold values from -6 to 6
- b_weight: bfloat16 [2, 8192, 128], P('kv'), may hold values from -0.0625 to 0.0625
Outputs:
- grad_c: bfloat16 [2048, 1024], P('seq', 'kv')
- grad_wb: float32 [2, 8192, 128], P('kv', 'seq')
Inputs may be any that keep to these rules, and one draw needn't show every extreme that they name: Each value appears once: plan[d] is the block of 128 consecutive positions held by index d of seq.
All inputs are finite; a program needn't handle non-finite values.
Results may differ from a plain program's by a relative error of at most 0.0049.
Values may be sent and summed in bfloat16 or wider, within the bound.
A program may use at most 64 MiB of HBM per device.

v0:
```python
import math
import jax
import jax.numpy as jnp
from jax import lax
from jax.sharding import PartitionSpec as P

NEG_FILL = -1e30


def block_sweep(update, running, pieces, shard_rows):
    total_rows = pieces[0].shape[0]
    shard_count = total_rows // shard_rows
    block_limit = max(1, 1024 // shard_rows)
    factor = 1
    for option in range(1, shard_count + 1):
        if shard_count % option == 0 and option <= block_limit:
            factor = option
    block_rows = factor * shard_rows
    block_count = total_rows // block_rows
    stacked = tuple(
        (member.reshape((block_count, block_rows) + member.shape[1:]) for member in pieces)
    )
    offsets = block_rows * jnp.arange(block_count, dtype=jnp.int32)

    def advance(partial_state, inputs):
        return (update(partial_state, inputs[0], inputs[1]), None)

    running, unused = lax.scan(advance, running, (stacked, offsets))
    return running


def local(plan, queries, keys, student_c, layer_input, b_weight):
    shard_rows = keys.shape[0]
    state_width = keys.shape[1]
    head_count = queries.shape[1] // state_width
    seq_count = lax.axis_size("seq")
    token_count = shard_rows * seq_count
    student_scale = 2.0 / math.sqrt(token_count)
    score_scale = 1.0 / math.sqrt(state_width)
    block_ids = jnp.arange(seq_count, dtype=jnp.int32)

    def positions_of(global_rows):
        owner_ids = global_rows // shard_rows
        picked = jnp.sum(
            jnp.where(owner_ids[:, None] == block_ids[None, :], plan[None, :], 0), axis=1
        )
        return picked * shard_rows + global_rows % shard_rows

    own_start = lax.axis_index("seq") * shard_rows
    query_pos = positions_of(own_start + jnp.arange(shard_rows, dtype=jnp.int32))
    query_heads = queries.reshape(shard_rows, head_count, state_width)
    student_heads = student_c.reshape(shard_rows, head_count, state_width)
    features = lax.all_gather(layer_input, "kv", axis=1, tiled=True)
    b_local = jnp.dot(features, b_weight[0], preferred_element_type=jnp.float32).astype(
        jnp.bfloat16
    )

    def scores_of(key_block, offset):
        key_pos = positions_of(offset + jnp.arange(key_block.shape[0], dtype=jnp.int32))
        visible = key_pos[None, None, :] <= query_pos[:, None, None]
        scores = (
            jnp.einsum("qhd,kd->qhk", query_heads, key_block, preferred_element_type=jnp.float32)
            * score_scale
        )
        return (jnp.where(visible, scores, NEG_FILL), visible)

    def stats_step(running, members, offset):
        highest, totals = running
        scores, visible = scores_of(members[0], offset)
        raised = jnp.maximum(highest, jnp.max(scores, axis=-1))
        weights = jnp.where(visible, jnp.exp(scores - raised[..., None]), 0.0)
        return (raised, totals * jnp.exp(highest - raised) + jnp.sum(weights, axis=-1))

    def pair_step(highest, totals):

        def advance_pair(running, members, offset):
            grad_acc, db_buffer = running
            key_block, b_block = members
            scores, visible = scores_of(key_block, offset)
            teacher = jnp.where(
                visible, jnp.exp(scores - highest[..., None]) / totals[..., None], 0.0
            )
            student = student_scale * jnp.einsum(
                "qhd,kd->qhk", student_heads, b_block, preferred_element_type=jnp.float32
            )
            residual = jnp.where(visible, student - teacher, 0.0).astype(jnp.bfloat16)
            grad_acc = grad_acc + jnp.einsum(
                "qhk,kd->qhd", residual, b_block, preferred_element_type=jnp.float32
            )
            contrib = jnp.einsum(
                "qhk,qhd->kd", residual, student_heads, preferred_element_type=jnp.float32
            )
            db_buffer = lax.dynamic_update_slice_in_dim(db_buffer, contrib, offset, 0)
            return (grad_acc, db_buffer)

        return advance_pair

    stats_init = (
        jnp.full((shard_rows, head_count), NEG_FILL, jnp.float32),
        jnp.zeros((shard_rows, head_count), jnp.float32),
    )
    pair_init = (
        jnp.zeros((shard_rows, head_count, state_width), jnp.float32),
        jnp.zeros((token_count, state_width), jnp.float32),
    )
    highest, totals = block_sweep(
        stats_step, stats_init, (lax.all_gather(keys, "seq", axis=0, tiled=True),), shard_rows
    )
    advance_pair = pair_step(highest, totals)
    grad_acc, db_buffer = block_sweep(
        advance_pair,
        pair_init,
        (
            lax.all_gather(keys, "seq", axis=0, tiled=True),
            lax.all_gather(b_local, "seq", axis=0, tiled=True),
        ),
        shard_rows,
    )
    arrived = lax.all_to_all(
        db_buffer.reshape(seq_count, shard_rows, state_width).astype(jnp.bfloat16),
        "seq",
        split_axis=0,
        concat_axis=0,
        tiled=True,
    ).astype(jnp.float32)
    b_grad = jnp.sum(arrived, axis=0).astype(jnp.bfloat16)
    weight_grad = lax.psum_scatter(
        jnp.einsum("td,tn->dn", features, b_grad, preferred_element_type=jnp.float32),
        "seq",
        scatter_dimension=0,
        tiled=True,
    )
    grad_c = grad_acc.reshape(shard_rows, head_count * state_width).astype(jnp.bfloat16)
    return (grad_c, weight_grad[None])


def solution(mesh):
    in_specs = (
        P(),
        P("seq", "kv"),
        P("seq", "kv"),
        P("seq", "kv"),
        P("seq", "kv"),
        P("kv", None, None),
    )
    out_specs = (P("seq", "kv"), P("kv", "seq", None))
    return jax.shard_map(local, mesh=mesh, in_specs=in_specs, out_specs=out_specs, check_vma=False)
```

profile of v0, /device:TPU:0, one launch (start us, length us, event | category | flops | bytes accessed | tf_op | source)
XLA Modules:
  0.0 205.9 jit_solution(17083190945803974519)
XLA Ops:
  7.2 0.0 copy-start
  7.2 0.0 copy-start.3
  7.2 0.0 copy-start.2
  7.2 0.0 all-gather.2.cloned.1.call-start
  7.2 0.7 all-gather.2.cloned.1.call-update
  7.9 0.0 reduce-scatter.2.cloned.1.call-start
  8.0 0.5 iota_multiply_fusion
  8.5 0.7 select_reduce_fusion.3
  9.3 26.4 %all_gather.12 = bf16[2048,128]{1,0:T(8,128)(2,1)} all-gather(bf16[128,128]{1,0:T(8,128)(2,1)} %param.12), channel_id=1, replica_groups=mesh['seq'=16,'kv'=2] {'seq'}, dimensions={0}, use_global_device_ids=true | all-gather | bytes 557056 | tf_op jit(solution)/shard_map/all_gather | solution.py:114
  35.6 1.0 copy.21
  36.7 0.8 copy.24
  37.5 0.0 copy-done.2
  37.5 0.1 copy.20
  37.6 0.1 copy.23
  37.7 0.0 copy-done.3
  37.7 15.4 %while.30 = (s32[]{:T(128)}, f32[128,4]{0,1:T(4,128)S(1)}, f32[128,4]{0,1:T(4,128)S(1)}, s32[2]{0:T(128)}, s32[16]{0:T(128)S(1)}, /*index=5*/s32[128]{0:T(128)S(...) while((s32[]{:T(128)}, f32[128,4]{0,1:T(4,128)S(1)}, ...), condition=%wide.region_5.6_spmd.clone, body=%wide.region_1.5_spmd.clone.sunk | while | flops 138624512 | bytes 5033156 | solution.py:28
  37.7 1.2 dynamic_slice.62
  38.9 0.6 add_select_fusion.6
  39.6 0.1 select_reduce_fusion.7
  39.7 0.6 fusion.70
  40.3 0.2 broadcast_compare_fusion.4
  40.5 2.8 %fusion.71 = (f32[128,4]{0,1:T(4,128)S(1)}, f32[1024,128,4]{1,0,2:T(8,128)}) fusion(pred[128,1024]{0,1:T(8,128)(4,1)S(1)} %broadcast_compare_fusion.4, bf16[128,4,128]{2,0,1:T(8,128)(2,1)} %get-tuple-element.599, bf16[2,1024,128]{2,1,0:T(8,128)(2,1)} %get-tuple-element.598, s32[]{:T(128)} %get-tuple-element.582), kind=kOutput, calls=%fused_computation.4.clone.1 | convolution fusion | flops 135790080 | bytes 2624000 | tf_op jit(solution)/shard_map/while/body/eval_jaxpr/qhd,kd->qhk/dot_general | solution.py:62
  43.3 2.1 %select_reduce_fusion.8 = f32[128,4]{0,1:T(4,128)S(1)} fusion(f32[1024,128,4]{1,0,2:T(8,128)} %get-tuple-element.559, f32[128,4]{0,1:T(4,128)S(1)} %select_maximum_fusion.2, pred[128,1024]{0,1:T(8,128)(4,1)S(1)} %broadcast_compare_fusion.4), kind=kLoop, calls=%fused_computation.3.clone.1 | loop fusion | flops 2620928 | bytes 2232320 | tf_op jit(solution)/shard_map/while/body/eval_jaxpr/reduce_sum | solution.py:72
  45.4 1.2 dynamic_slice.62
  46.6 0.6 add_select_fusion.6
  47.3 0.1 select_reduce_fusion.7
  47.3 0.6 fusion.70
  48.0 0.2 broadcast_compare_fusion.4
  48.2 2.8 %fusion.71 = (f32[128,4]{0,1:T(4,128)S(1)}, f32[1024,128,4]{1,0,2:T(8,128)}) fusion(pred[128,1024]{0,1:T(8,128)(4,1)S(1)} %broadcast_compare_fusion.4, bf16[128,4,128]{2,0,1:T(8,128)(2,1)} %get-tuple-element.599, bf16[2,1024,128]{2,1,0:T(8,128)(2,1)} %get-tuple-element.598, s32[]{:T(128)} %get-tuple-element.582), kind=kOutput, calls=%fused_computation.4.clone.1 | convolution fusion | flops 135790080 | bytes 2624000 | tf_op jit(solution)/shard_map/while/body/eval_jaxpr/qhd,kd->qhk/dot_general | solution.py:62
  51.0 2.1 %select_reduce_fusion.8 = f32[128,4]{0,1:T(4,128)S(1)} fusion(f32[1024,128,4]{1,0,2:T(8,128)} %get-tuple-element.559, f32[128,4]{0,1:T(4,128)S(1)} %select_maximum_fusion.2, pred[128,1024]{0,1:T(8,128)(4,1)S(1)} %broadcast_compare_fusion.4), kind=kLoop, calls=%fused_computation.3.clone.1 | loop fusion | flops 2620928 | bytes 2232320 | tf_op jit(solution)/shard_map/while/body/eval_jaxpr/reduce_sum | solution.py:72
  53.1 0.0 all-gather.2.cloned.1.call-done
  53.2 0.0 copy-done
  53.2 2.3 %fusion.41 = bf16[128,128]{1,0:T(8,128)(2,1)S(1)} fusion(bf16[128,8192]{1,0:T(8,128)(2,1)} %all-gather.2.cloned.1.call-done, bf16[1,8192,128]{2,1,0:T(8,128)(2,1)S(1)} %copy-done), kind=kOutput, calls=%fused_computation.67 | convolution fusion | flops 268451840 | bytes 4227072 | tf_op jit(solution)/shard_map/dot_general | solution.py:54
  55.5 20.3 %all_gather.11 = bf16[2048,128]{1,0:T(8,128)(2,1)} all-gather(bf16[128,128]{1,0:T(8,128)(2,1)S(1)} %fusion.41), channel_id=1, replica_groups=mesh['seq'=16,'kv'=2] {'seq'}, dimensions={0}, use_global_device_ids=true | all-gather | bytes 557056 | tf_op jit(solution)/shard_map/all_gather | solution.py:115
  75.7 0.9 broadcast_in_dim.132
  76.6 26.1 %while.31 = (s32[]{:T(128)}, f32[128,4,128]{2,0,1:T(8,128)}, bf16[2048,128]{1,0:T(8,128)(2,1)}, s32[2]{0:T(128)}, s32[16]{0:T(128)S(1)}, /*index=5*/s32[128]{0:T...) while((s32[]{:T(128)}, f32[128,4,128]{2,0,1:T(8,128)}, ...), condition=%wide.region_8.9_spmd.clone, body=%wide.region_6.8_spmd.clone.sunk | while | flops 541930496 | bytes 10123537 | solution.py:28
  76.6 1.3 dynamic_slice.66
  77.8 0.6 add_select_fusion.7
  78.5 0.1 select_reduce_fusion.9
  78.6 0.6 fusion.82
  79.2 0.2 broadcast_compare_fusion.5
  79.4 1.4 fusion.81
  80.8 2.0 fusion.83
  82.8 0.4 convolution_bitcast_fusion.3
  85.2 2.7 %dynamic_update_slice.8 = bf16[2048,128]{1,0:T(8,128)(2,1)} dynamic-update-slice(bf16[2048,128]{1,0:T(8,128)(2,1)} %get-tuple-element.619, bf16[1024,128]{1,0:T(8,128)(2,1)S(1)} %convolution_bitcast_fusion.3, s32[]{:T(128)S(6)} %select_n.206, s32[]{:T(128)} %constant.191.clone.1..sunk.1) | dynamic-update-slice | bytes 524292 | tf_op jit(solution)/shard_map/while/body/eval_jaxpr/dynamic_update_slice | solution.py:93
  87.9 2.1 %convolution_add_fusion.2 = f32[128,4,128]{2,0,1:T(8,128)} fusion(bf16[128,4,1024]{0,2,1:T(8,128)(2,1)S(1)} %fusion.83, f32[128,4,128]{2,0,1:T(8,128)} %get-tuple-element.618, bf16[2,1024,128]{2,1,0:T(8,128)(2,1)} %get-tuple-element.638, s32[]{:T(128)} %get-tuple-element.617, pred[]{:T(512)S(6)} %compare.39), kind=kOutput, calls=%fused_computation.37.clone.1 | convolution fusion | flops 134348800 | bytes 1835521 | tf_op jit(solution)/shard_map/while/body/eval_jaxpr/qhk,kd->qhd/dot_general | solution.py:87
  90.1 1.3 dynamic_slice.66
  91.3 0.6 add_select_fusion.7
  92.0 0.1 select_reduce_fusion.9
  92.1 0.6 fusion.82
  92.7 0.2 broadcast_compare_fusion.5
  92.9 1.4 fusion.81
  94.3 2.0 fusion.83
  96.3 0.4 convolution_bitcast_fusion.3
  98.7 1.8 dynamic_update_slice.8
  100.5 2.2 %convolution_add_fusion.2 = f32[128,4,128]{2,0,1:T(8,128)} fusion(bf16[128,4,1024]{0,2,1:T(8,128)(2,1)S(1)} %fusion.83, f32[128,4,128]{2,0,1:T(8,128)} %get-tuple-element.618, bf16[2,1024,128]{2,1,0:T(8,128)(2,1)} %get-tuple-element.638, s32[]{:T(128)} %get-tuple-element.617, pred[]{:T(512)S(6)} %compare.39), kind=kOutput, calls=%fused_computation.37.clone.1 | convolution fusion | flops 134348800 | bytes 1835521 | tf_op jit(solution)/shard_map/while/body/eval_jaxpr/qhk,kd->qhd/dot_general | solution.py:87
  102.7 18.0 %all_to_all.5 = bf16[16,128,128]{2,1,0:T(8,128)(2,1)S(1)} all-to-all(bf16[16,128,128]{2,1,0:T(8,128)(2,1)} %bitcast.107), channel_id=1, replica_groups=mesh['seq'=16,'kv'=2] {'seq'}, dimensions={0} | all-to-all | bytes 1048576 | tf_op jit(solution)/shard_map/all_to_all | solution.py:119
  120.7 0.1 reduce_sum.58
  120.8 4.2 %convolution_bitcast_fusion.1 = f32[8192,128]{0,1:T(8,128)} fusion(bf16[128,128]{1,0:T(8,128)(2,1)S(1)} %reduce_sum.58, bf16[128,8192]{1,0:T(8,128)(2,1)} %all-gather.2.cloned.1.call-done), kind=kOutput, calls=%fused_computation.64 | convolution fusion | flops 268435456 | bytes 6324224 | tf_op jit(solution)/shard_map/td,tn->dn/dot_general | solution.py:128
  125.0 0.0 reduce-scatter.2.cloned.1.call-update
  125.0 0.9 copy-done.1
  126.0 0.7 copy_bitcast_fusion
  126.6 70.7 %reduce-scatter.2.cloned.1.call-done = f32[512,128]{0,1:T(8,128)} async-done(((f32[8192,128]{0,1:T(8,128)}), f32[512,128]{0,1:T(8,128)}) %reduce-scatter.2.cloned.1.call-update) | async-done | bytes 262160 | tf_op jit(solution)/shard_map/reduce_scatter | solution.py:127
  197.3 1.8 copy.26
  (12 shorter events, 0.1 us)
Async XLA Ops:
  7.2 46.0 %copy-start = (bf16[1,8192,128]{2,1,0:T(8,128)(2,1)S(1)}, bf16[1,8192,128]{2,1,0:T(8,128)(2,1)}, u32[]{:S(2)}) copy-start(bf16[1,8192,128]{2,1,0:T(8,128)(2,1)} %param.15) | copy-start | bytes 6291460
  7.2 30.5 %copy-start.3 = (s32[16]{0:T(128)S(1)}, s32[16]{0:T(128)}, u32[]{:S(2)}) copy-start(s32[16]{0:T(128)} %param.10) | copy-start | bytes 196
  7.2 30.3 %copy-start.2 = (bf16[128,512]{1,0:T(8,128)(2,1)S(1)}, bf16[128,512]{1,0:T(8,128)(2,1)}, u32[]{:S(2)}) copy-start(bf16[128,512]{1,0:T(8,128)(2,1)} %param.13) | copy-start | bytes 393220
  7.2 45.9 %all-gather.2.cloned.1.call-start = ((), (), s32[]{:S(2)}) async-start(), calls=%async_computation.2 | async-start | bytes 3145728 | tf_op jit(solution)/shard_map/all_gather | solution.py:53
  7.9 189.4 %reduce-scatter.2.cloned.1.call-start = ((), (), s32[]{:S(2)}) async-start(), calls=%async_computation.3 | async-start | bytes 4456448 | tf_op jit(solution)/shard_map/reduce_scatter | solution.py:127
  125.0 0.9 copy-start.1
Sparse Core Ops, SparseCore 0:
  9.6 35.7 all-gather.1
  125.2 72.1 reduce-scatter.1
where the time goes:
time: 207 us; the launch traced here: 206 us
  waiting for transfers between devices  71.4 us (34%)
  blocking collectives  64.6 us (31%)
  matrix products  24.1 us (12%)
  local copies, waits for them, and re-layouts  15.1 us (7%)
  between operations  14.1 us (7%)
  other arithmetic  12.5 us (6%)
  loops' own time  4.02 us (2%)
    reduce_scatter x1, waiting for transfers between devices, local(): lax.psum_scatter(jnp.einsum('td,tn->dn', features, b_grad, preferred_elem...  70.7 us
    all_gather x1, blocking collectives, local(): lax.all_gather(keys, 'seq', axis=0, tiled=True)  26.4 us
    all_gather x1, blocking collectives, local(): lax.all_gather(b_local, 'seq', axis=0, tiled=True)  20.3 us
    all_to_all x1, blocking collectives, local(): lax.all_to_all(db_buffer.reshape(seq_count, shard_rows, state_width).asty...  18 us
    dot_general x4, matrix products, scores_of(): jnp.einsum('qhd,kd->qhk', query_heads, key_block, preferred_element_type=...  9.57 us
    dynamic_slice x4, local copies, waits for them, and re-layouts, block_sweep(): running, unused = lax.scan(advance, running, (stacked, offsets))  4.89 us
    unnamed x13, local copies, waits for them, and re-layouts  4.78 us
    dynamic_update_slice x2, local copies, waits for them, and re-layouts, advance_pair(): db_buffer = lax.dynamic_update_slice_in_dim(db_buffer, contrib, offset, 0)  4.53 us
  transfers between devices with their start and end apart: 2, of which 1 were waited for; matrix products, arithmetic and copies ran while one was open for 9% of the time, Pallas kernels for 0%

commit v1 on v0

--- a/solution.py
+++ b/solution.py
@@ -5,6 +5,27 @@
 from jax.sharding import PartitionSpec as P
 
 NEG_FILL = -1e30
+
+
+def laid_out(parts, dim):
+    parts = jnp.moveaxis(parts, 0, dim)
+    dims = parts.shape
+    return parts.reshape(*dims[:dim], dims[dim] * dims[dim + 1], *dims[dim + 2 :])
+
+
+def collected_by_bits(array, axis):
+    size, index = (lax.axis_size(axis), lax.axis_index(axis))
+    parts, bit = (array[None], 1)
+    while bit < size:
+        received = lax.ppermute(parts, axis, [(i, i ^ bit) for i in range(size)])
+        low = index & bit == 0
+        parts = jnp.concatenate([jnp.where(low, parts, received), jnp.where(low, received, parts)])
+        bit *= 2
+    return parts
+
+
+def collect(x, axis, dim):
+    return laid_out(collected_by_bits(x, axis), dim)
 
 
 def block_sweep(update, running, pieces, shard_rows):
@@ -110,10 +131,7 @@
     grad_acc, db_buffer = block_sweep(
         advance_pair,
         pair_init,
-        (
-            lax.all_gather(keys, "seq", axis=0, tiled=True),
-            lax.all_gather(b_local, "seq", axis=0, tiled=True),
-        ),
+        (collect(keys, "seq", 0), lax.all_gather(b_local, "seq", axis=0, tiled=True)),
         shard_rows,
     )
     arrived = lax.all_to_all(

time: 207 us -> 217 us (1.048)
  waiting for transfers between devices: 71.4 us -> 77.6 us
  other arithmetic: 12.5 us -> 15.9 us
    ppermute x0 -> x4, waiting for transfers between devices: none -> 7.11 us  [collected_by_bits(): received = lax.ppermute(parts, axis, [(i, i ^ bit) for i in range(size)])]
    all_gather x1, blocking collectives: 20.3 us -> 22.5 us  [local(): lax.all_gather(b_local, 'seq', axis=0, tiled=True)]
    unnamed x13 -> x15, local copies, waits for them, and re-layouts: 4.78 us -> 4.78 us
  transfers between devices with their start and end apart: 2 -> 6, of which waited for: 1 -> 3; matrix products, arithmetic and copies ran while one was open for 9% -> 11% of each run, Pallas kernels for 0% -> 0%
where the time goes in v1:
time: 217 us; the launch traced here: 216 us
  waiting for transfers between devices  77.6 us (36%)
  blocking collectives  65.3 us (30%)
  matrix products  23.8 us (11%)
  other arithmetic  15.9 us (7%)
  local copies, waits for them, and re-layouts  15.2 us (7%)
  between operations  14.2 us (7%)
  loops' own time  3.45 us (2%)
    reduce_scatter x1, waiting for transfers between devices, local(): lax.psum_scatter(jnp.einsum('td,tn->dn', features, b_grad, preferred_elem...  70.3 us
    all_gather x1, blocking collectives, local(): lax.all_gather(keys, 'seq', axis=0, tiled=True)  24.8 us
    all_gather x1, blocking collectives, local(): lax.all_gather(b_local, 'seq', axis=0, tiled=True)  22.5 us
    all_to_all x1, blocking collectives, local(): lax.all_to_all(db_buffer.reshape(seq_count, shard_rows, state_width).asty...  18 us
    dot_general x4, matrix products, scores_of(): jnp.einsum('qhd,kd->qhk', query_heads, key_block, preferred_element_type=...  9.25 us
    ppermute x4, waiting for transfers between devices, collected_by_bits(): received = lax.ppermute(parts, axis, [(i, i ^ bit) for i in range(size)])  7.11 us
    dynamic_slice x4, local copies, waits for them, and re-layouts, block_sweep(): running, unused = lax.scan(advance, running, (stacked, offsets))  5.04 us
    unnamed x15, local copies, waits for them, and re-layouts  4.78 us
  transfers between devices with their start and end apart: 6, of which 3 were waited for; matrix products, arithmetic and copies ran while one was open for 11% of the time, Pallas kernels for 0%

profile of v1, /device:TPU:0, one launch (start us, length us, event | category | flops | bytes accessed | tf_op | source)
XLA Modules:
  0.0 216.3 jit_solution(10526204895149403873)
XLA Ops:
  7.2 0.5 collective-permute-start
  7.8 0.2 all-gather.2.cloned.1.call-update
  8.0 24.8 %all_gather.11 = bf16[2048,128]{1,0:T(8,128)(2,1)S(1)} all-gather(bf16[128,128]{1,0:T(8,128)(2,1)} %param.12), channel_id=1, replica_groups=mesh['seq'=16,'kv'=2] {'seq'}, dimensions={0}, use_global_device_ids=true | all-gather | bytes 557056 | tf_op jit(solution)/shard_map/all_gather | solution.py:128
  32.8 0.8 broadcast_select_fusion.7
  33.6 0.1 collective-permute-start.1
  33.7 0.7 select_reduce_fusion.3
  34.4 3.6 %collective-permute-done.1 = bf16[2,128,128]{2,1,0:T(8,128)(2,1)S(1)} collective-permute-done((bf16[2,128,128]{2,1,0:T(8,128)(2,1)S(1)}, bf16[2,128,128]{2,1,0:T(8,128)(2,1)S(1)}, u32[]{:S(2)}, u32[]{:S(2)}) %collective-permute-start.1) | collective-permute-done | bytes 65568 | tf_op jit(solution)/shard_map/ppermute | solution.py:20
  38.0 0.1 collective-permute-start.2
  38.2 0.1 copy.21
  38.3 0.8 copy.24
  39.1 0.6 iota_multiply_fusion
  39.6 3.5 %collective-permute-done.2 = bf16[4,128,128]{2,1,0:T(8,128)(2,1)S(1)} collective-permute-done((bf16[4,128,128]{2,1,0:T(8,128)(2,1)S(1)}, bf16[4,128,128]{2,1,0:T(8,128)(2,1)S(1)}, u32[]{:S(2)}, u32[]{:S(2)}) %collective-permute-start.2) | collective-permute-done | bytes 131104 | tf_op jit(solution)/shard_map/ppermute | solution.py:20
  43.2 0.1 collective-permute-start.3
  43.3 17.2 %while.30 = (s32[]{:T(128)}, f32[128,4]{0,1:T(4,128)S(1)}, f32[128,4]{0,1:T(4,128)}, s32[2]{0:T(128)}, s32[16]{0:T(128)S(1)}, /*index=5*/s32[128]{0:T(128)S(1)},...) while((s32[]{:T(128)}, f32[128,4]{0,1:T(4,128)S(1)}, ...), condition=%wide.region_5.6_spmd.clone, body=%wide.region_1.5_spmd.clone.sunk | while | flops 138624512 | bytes 5032648 | solution.py:49
  43.3 1.3 dynamic_slice.62
  44.6 0.6 add_select_fusion.6
  45.2 0.1 select_reduce_fusion.7
  45.3 0.6 fusion.70
  45.9 0.2 broadcast_compare_fusion.4
  46.1 2.7 %fusion.71 = (f32[128,4]{0,1:T(4,128)S(1)}, f32[1024,128,4]{1,0,2:T(8,128)}) fusion(pred[128,1024]{0,1:T(8,128)(4,1)S(1)} %broadcast_compare_fusion.4, bf16[128,4,128]{2,0,1:T(8,128)(2,1)} %get-tuple-element.607, bf16[2,1024,128]{2,1,0:T(8,128)(2,1)S(1)} %get-tuple-element.606, s32[]{:T(128)} %get-tuple-element.590), kind=kOutput, calls=%fused_computation.4.clone.1 | convolution fusion | flops 135790080 | bytes 2623492 | tf_op jit(solution)/shard_map/while/body/eval_jaxpr/qhd,kd->qhk/dot_general | solution.py:83
  48.8 2.1 select_reduce_fusion.8
  51.0 0.6 fusion.72
  51.6 1.2 dynamic_slice.62
  52.8 0.6 add_select_fusion.6
  53.5 0.1 select_reduce_fusion.7
  53.5 0.6 fusion.70
  54.2 0.2 broadcast_compare_fusion.4
  54.4 2.7 %fusion.71 = (f32[128,4]{0,1:T(4,128)S(1)}, f32[1024,128,4]{1,0,2:T(8,128)}) fusion(pred[128,1024]{0,1:T(8,128)(4,1)S(1)} %broadcast_compare_fusion.4, bf16[128,4,128]{2,0,1:T(8,128)(2,1)} %get-tuple-element.607, bf16[2,1024,128]{2,1,0:T(8,128)(2,1)S(1)} %get-tuple-element.606, s32[]{:T(128)} %get-tuple-element.590), kind=kOutput, calls=%fused_computation.4.clone.1 | convolution fusion | flops 135790080 | bytes 2623492 | tf_op jit(solution)/shard_map/while/body/eval_jaxpr/qhd,kd->qhk/dot_general | solution.py:83
  57.1 2.1 select_reduce_fusion.8
  59.2 1.3 fusion.72
  60.5 1.0 copy.20
  61.5 0.1 copy.23
  61.7 0.8 pad_maximum_fusion
  62.6 2.3 %fusion.41 = bf16[128,128]{1,0:T(8,128)(2,1)S(1)} fusion(bf16[128,8192]{1,0:T(8,128)(2,1)} %all-gather.2.cloned.1.call-done, bf16[1,8192,128]{2,1,0:T(8,128)(2,1)S(1)} %copy-done), kind=kOutput, calls=%fused_computation.67 | convolution fusion | flops 268451840 | bytes 4227072 | tf_op jit(solution)/shard_map/dot_general | solution.py:75
  64.9 22.5 %all_gather.10 = bf16[2048,128]{1,0:T(8,128)(2,1)} all-gather(bf16[128,128]{1,0:T(8,128)(2,1)S(1)} %fusion.41), channel_id=1, replica_groups=mesh['seq'=16,'kv'=2] {'seq'}, dimensions={0}, use_global_device_ids=true | all-gather | bytes 557056 | tf_op jit(solution)/shard_map/all_gather | solution.py:134
  87.3 0.9 broadcast_in_dim.135
  88.2 25.1 %while.31 = (s32[]{:T(128)}, f32[128,4,128]{2,0,1:T(8,128)}, bf16[2048,128]{1,0:T(8,128)(2,1)}, s32[2]{0:T(128)}, s32[16]{0:T(128)S(1)}, /*index=5*/s32[128]{0:T...) while((s32[]{:T(128)}, f32[128,4,128]{2,0,1:T(8,128)}, ...), condition=%wide.region_8.9_spmd.clone, body=%wide.region_6.8_spmd.clone.sunk | while | flops 541930496 | bytes 12220209 | solution.py:49
  88.2 1.3 dynamic_slice.66
  89.5 0.6 add_select_fusion.7
  90.0 0.1 select_reduce_fusion.9
  90.1 0.6 fusion.82
  90.7 0.2 broadcast_compare_fusion.5
  90.9 1.4 fusion.81
  92.3 1.9 fusion.83
  94.2 0.4 convolution_bitcast_fusion.3
  96.3 2.7 %dynamic_update_slice.8 = bf16[2048,128]{1,0:T(8,128)(2,1)} dynamic-update-slice(bf16[2048,128]{1,0:T(8,128)(2,1)} %get-tuple-element.627, bf16[1024,128]{1,0:T(8,128)(2,1)S(1)} %convolution_bitcast_fusion.3, s32[]{:T(128)S(6)} %select_n.282, s32[]{:T(128)} %constant.195.clone.1..sunk.1) | dynamic-update-slice | bytes 524292 | tf_op jit(solution)/shard_map/while/body/eval_jaxpr/dynamic_update_slice | solution.py:114
  99.1 2.1 convolution_add_fusion.2
  101.2 1.3 dynamic_slice.66
  102.5 0.6 add_select_fusion.7
  103.0 0.1 select_reduce_fusion.9
  103.1 0.6 fusion.82
  103.7 0.2 broadcast_compare_fusion.5
  103.9 1.4 fusion.81
  105.3 1.9 fusion.83
  107.2 0.4 convolution_bitcast_fusion.3
  109.3 1.8 dynamic_update_slice.8
  111.1 2.2 %convolution_add_fusion.2 = f32[128,4,128]{2,0,1:T(8,128)} fusion(bf16[128,4,1024]{0,2,1:T(8,128)(2,1)S(1)} %fusion.83, f32[128,4,128]{2,0,1:T(8,128)} %get-tuple-element.626, bf16[2,1024,128]{2,1,0:T(8,128)(2,1)} %get-tuple-element.646, s32[]{:T(128)} %get-tuple-element.625, pred[]{:T(512)S(6)} %compare.39), kind=kOutput, calls=%fused_computation.37.clone.1 | convolution fusion | flops 134348800 | bytes 1835521 | tf_op jit(solution)/shard_map/while/body/eval_jaxpr/qhk,kd->qhd/dot_general | solution.py:108
  113.3 18.0 %all_to_all.5 = bf16[16,128,128]{2,1,0:T(8,128)(2,1)S(1)} all-to-all(bf16[16,128,128]{2,1,0:T(8,128)(2,1)} %bitcast.112), channel_id=1, replica_groups=mesh['seq'=16,'kv'=2] {'seq'}, dimensions={0} | all-to-all | bytes 1048576 | tf_op jit(solution)/shard_map/all_to_all | solution.py:137
  131.3 0.1 reduce_sum.58
  131.4 4.3 %convolution_bitcast_fusion.1 = f32[8192,128]{0,1:T(8,128)} fusion(bf16[128,128]{1,0:T(8,128)(2,1)S(1)} %reduce_sum.58, bf16[128,8192]{1,0:T(8,128)(2,1)} %all-gather.2.cloned.1.call-done), kind=kOutput, calls=%fused_computation.64 | convolution fusion | flops 268435456 | bytes 6324224 | tf_op jit(solution)/shard_map/td,tn->dn/dot_general | solution.py:146
  135.7 0.9 copy-done.1
  136.6 0.7 copy_bitcast_fusion
  137.3 70.3 %reduce-scatter.2.cloned.1.call-done = f32[512,128]{0,1:T(8,128)} async-done(((f32[8192,128]{0,1:T(8,128)}), f32[512,128]{0,1:T(8,128)}) %reduce-scatter.2.cloned.1.call-update) | async-done | bytes 262160 | tf_op jit(solution)/shard_map/reduce_scatter | solution.py:145
  207.6 1.8 copy.26
  (34 shorter events, 0.3 us)
Async XLA Ops:
  7.2 55.4 %copy-start = (bf16[1,8192,128]{2,1,0:T(8,128)(2,1)S(1)}, bf16[1,8192,128]{2,1,0:T(8,128)(2,1)}, u32[]{:S(2)}) copy-start(bf16[1,8192,128]{2,1,0:T(8,128)(2,1)} %param.15) | copy-start | bytes 6291460
  7.2 36.1 %copy-start.4 = (s32[16]{0:T(128)S(1)}, s32[16]{0:T(128)}, u32[]{:S(2)}) copy-start(s32[16]{0:T(128)} %param.10) | copy-start | bytes 196
  7.2 31.0 %copy-start.3 = (bf16[128,512]{1,0:T(8,128)(2,1)S(1)}, bf16[128,512]{1,0:T(8,128)(2,1)}, u32[]{:S(2)}) copy-start(bf16[128,512]{1,0:T(8,128)(2,1)} %param.11) | copy-start | bytes 393220
  7.2 55.4 %all-gather.2.cloned.1.call-start = ((), (), s32[]{:S(2)}) async-start(), calls=%async_computation.2 | async-start | bytes 3145728 | tf_op jit(solution)/shard_map/all_gather | solution.py:74
  7.2 25.6 %collective-permute-start = (bf16[1,128,128]{2,1,0:T(8,128)(2,1)}, bf16[1,128,128]{2,1,0:T(8,128)(2,1)S(1)}, u32[]{:S(2)}, u32[]{:S(2)}) collective-permute-start(bf16[1,128,128]{2,1,0:T(8,128)(2,1)} %bitcast.117), channel_id=1, source_target_pairs={{0,2},{2,0},{4,6},{6,4},{8,10},{10,8},{12,14},{14,12},{16,18},{18,... | collective-permute-start | bytes 98312 | tf_op jit(solution)/shard_map/ppermute | solution.py:20
  7.9 199.7 %reduce-scatter.2.cloned.1.call-start = ((), (), s32[]{:S(2)}) async-start(), calls=%async_computation.3 | async-start | bytes 4456448 | tf_op jit(solution)/shard_map/reduce_scatter | solution.py:145
  33.6 4.4 %collective-permute-start.1 = (bf16[2,128,128]{2,1,0:T(8,128)(2,1)S(1)}, bf16[2,128,128]{2,1,0:T(8,128)(2,1)S(1)}, u32[]{:S(2)}, u32[]{:S(2)}) collective-permute-start(bf16[2,128,128]{2,1,0:T(8,128)(2,1)S(1)} %pad_maximum_fusion.3), channel_id=1, source_target_pairs={{0,4},{2,6},{4,0},{6,2},{8,12},{10,14},{12,8},{14,10},{16,20},{18,... | collective-permute-start | bytes 196616 | tf_op jit(solution)/shard_map/ppermute | solution.py:20
  38.0 5.1 %collective-permute-start.2 = (bf16[4,128,128]{2,1,0:T(8,128)(2,1)S(1)}, bf16[4,128,128]{2,1,0:T(8,128)(2,1)S(1)}, u32[]{:S(2)}, u32[]{:S(2)}) collective-permute-start(bf16[4,128,128]{2,1,0:T(8,128)(2,1)S(1)} %pad_maximum_fusion.2), channel_id=1, source_target_pairs={{0,8},{2,10},{4,12},{6,14},{8,0},{10,2},{12,4},{14,6},{16,24},{18,... | collective-permute-start | bytes 393224 | tf_op jit(solution)/shard_map/ppermute | solution.py:20
  43.2 18.4 %collective-permute-start.3 = (bf16[8,128,128]{2,1,0:T(8,128)(2,1)S(1)}, bf16[8,128,128]{2,1,0:T(8,128)(2,1)S(1)}, u32[]{:S(2)}, u32[]{:S(2)}) collective-permute-start(bf16[8,128,128]{2,1,0:T(8,128)(2,1)S(1)} %pad_maximum_fusion.1), channel_id=1, source_target_pairs={{0,16},{2,18},{4,20},{6,22},{8,24},{10,26},{12,28},{14,30},{16,0},... | collective-permute-start | bytes 786440 | tf_op jit(solution)/shard_map/ppermute | solution.py:20
  62.6 25.6 %copy-start.5 = (f32[128,4]{0,1:T(4,128)S(1)}, f32[128,4]{0,1:T(4,128)}, u32[]{:S(2)}) copy-start(f32[128,4]{0,1:T(4,128)} %get-tuple-element.621) | copy-start | bytes 6148
  88.2 4.1 %copy-start.2 = (bf16[2,1024,128]{2,1,0:T(8,128)(2,1)S(1)}, bf16[2,1024,128]{2,1,0:T(8,128)(2,1)}, u32[]{:S(2)}) copy-start(bf16[2,1024,128]{2,1,0:T(8,128)(2,1)} %get-tuple-element.648) | copy-start | bytes 1572868 | tf_op jit(solution)/shard_map/while
  101.2 4.1 %copy-start.2 = (bf16[2,1024,128]{2,1,0:T(8,128)(2,1)S(1)}, bf16[2,1024,128]{2,1,0:T(8,128)(2,1)}, u32[]{:S(2)}) copy-start(bf16[2,1024,128]{2,1,0:T(8,128)(2,1)} %get-tuple-element.648) | copy-start | bytes 1572868 | tf_op jit(solution)/shard_map/while
  135.7 0.9 copy-start.1
Sparse Core Ops, SparseCore 0:
  9.6 35.8 all-gather.1
  135.8 71.7 reduce-scatter.1
